TPU v7x, 32 devices: a whole 2x2x4 slice. The times are simulated.
32 devices in a mesh: blk: 16 (over z, x, core), head: 2 (over y).
Axes of the slice: x: 2, y: 2, z: 4, core: 2. Of those that a mesh axis runs over, the one named last changes fastest.
Arguments:
- query_rows: bfloat16 [8192, 1024], P('blk', 'head'), may hold values from -24 to 24
- key_rows: bfloat16 [8192, 128], P('blk'), may hold values from -9 to 9
- value_rows: bfloat16 [8192, 128], P('blk'), may hold values from -6 to 6
- grad_out: bfloat16 [8192, 1024], P('blk', 'head'), may hold values from -6 to 6
- subtree_end: int32 [8192], P('blk'), may hold values from 1 to 8192, as said below
Outputs:
- grad_queries: bfloat16 [8192, 1024], P('blk', 'head')
- grad_keys: bfloat16 [8192, 128], P(('blk', 'head'))
- grad_values: bfloat16 [8192, 128], P(('blk', 'head'))
Inputs may be any that keep to these rules, and one draw needn't show every extreme that they name: Tokens are packed depth-first in trees: j < subtree_end[j], any two subtrees are nested or apart, and j is an ancestor of i or i itself exactly when j <= i < subtree_end[j]. A tree holds at most 2048 tokens, so a token's ancestors lie at most 4 blocks of 512 positions before its own block; some token has its root exactly 4 blocks before its own.
All inputs are finite; a program needn't handle non-finite values.
Results may differ from a plain program's by a relative error of at most 0.0095.
Values may be sent and summed in bfloat16 or wider, within the bound.
A program may use at most 64 MiB of HBM per device.

v0:
```python
import functools
import math

import jax
import jax.numpy as jnp
from jax import lax
from jax.experimental import pallas as pl
from jax.experimental.pallas import tpu as pltpu
from jax.sharding import PartitionSpec as P

WINDOW = 4
NEGATIVE = -1e30
CHUNK = 256
NT = (((1,), (1,)), ((), ()))
NN = (((1,), (0,)), ((), ()))
TN = (((0,), (0,)), ((), ()))


def dot(a, b, dims):
    return lax.dot_general(a, b, dims, preferred_element_type=jnp.float32)


def stats_step(d, r, q0, first, tok, heads, dim, slope, q_ref, g_ref, kv_ref, ends_ref, e_ref, dp_ref, m_ref, l_ref, t_ref, mc_ref):
    blk = lax.axis_index("blk")
    qn = tok - q0
    row0 = r * CHUNK
    rows = pl.ds(row0, CHUNK) if isinstance(r, int) else pl.ds(pl.multiple_of(row0, CHUNK), CHUNK)
    base = d * tok + row0
    slab = pl.ds(base, CHUNK) if isinstance(r, int) else pl.ds(pl.multiple_of(base, CHUNK), CHUNK)
    keys = kv_ref[d, rows, 0:dim]
    values = kv_ref[d, rows, dim : 2 * dim]
    per = CHUNK // 128
    tiles = []
    for piece in range(per):
        line = ends_ref[d, pl.ds(r * per + piece, 1), :]
        tiles.append(jnp.broadcast_to(line, (128, 128)).T)
    ends = jnp.concatenate(tiles, axis=0)
    ends = jnp.where(blk >= d, ends - blk * tok, 0)
    spot = lax.broadcasted_iota(jnp.int32, (CHUNK, 128), 1) + q0
    key_spot = lax.broadcasted_iota(jnp.int32, (CHUNK, 128), 0) + (row0 - d * tok)
    bias = []
    for piece in range(qn // 128):
        here = spot + piece * 128
        ok = here < ends
        if d == 0:
            ok = ok & (key_spot <= here)
        bias.append(jnp.where(ok, 0.0, NEGATIVE))
    bias = jnp.concatenate(bias, axis=1)
    index = d * (tok // CHUNK) + r
    for h in range(heads):
        lanes = slice(h * dim, (h + 1) * dim)
        s = dot(keys, q_ref[q0:tok, lanes], NT) + bias
        dp = dot(values, g_ref[q0:tok, lanes], NT)
        top = jnp.max(s, axis=0, keepdims=True)
        if first:
            new = top
        else:
            old = m_ref[h : h + 1, q0:tok]
            new = jnp.maximum(old, top)
        e = jnp.exp2((s - new) * slope)
        total = jnp.sum(e, axis=0, keepdims=True)
        cross = jnp.sum(e * dp, axis=0, keepdims=True)
        if not first:
            fade = jnp.exp2((old - new) * slope)
            total = total + l_ref[h : h + 1, q0:tok] * fade
            cross = cross + t_ref[h : h + 1, q0:tok] * fade
        m_ref[h : h + 1, q0:tok] = new
        l_ref[h : h + 1, q0:tok] = total
        t_ref[h : h + 1, q0:tok] = cross
        mc_ref[index, h : h + 1, q0:tok] = new
        e_ref[slab, h * tok + q0 : (h + 1) * tok] = e.astype(jnp.bfloat16)
        dp_ref[slab, h * tok + q0 : (h + 1) * tok] = dp.astype(jnp.bfloat16)


def grads_step(d, r, q0, tok, heads, dim, slope, scale, q_ref, g_ref, kv_ref, e_ref, dp_ref, m_ref, l_ref, t_ref, mc_ref, dq_ref):
    row0 = r * CHUNK
    rows = pl.ds(row0, CHUNK) if isinstance(r, int) else pl.ds(pl.multiple_of(row0, CHUNK), CHUNK)
    base = d * tok + row0
    slab = pl.ds(base, CHUNK) if isinstance(r, int) else pl.ds(pl.multiple_of(base, CHUNK), CHUNK)
    keys = kv_ref[d, rows, 0:dim]
    index = d * (tok // CHUNK) + r
    dk = jnp.zeros((CHUNK, dim), jnp.float32)
    dv = jnp.zeros((CHUNK, dim), jnp.float32)
    for h in range(heads):
        lanes = slice(h * dim, (h + 1) * dim)
        cols = slice(h * tok + q0, (h + 1) * tok)
        unit = jnp.exp2((mc_ref[index, h : h + 1, q0:tok] - m_ref[h : h + 1, q0:tok]) * slope) * l_ref[h : h + 1, q0:tok]
        p = e_ref[slab, cols].astype(jnp.float32) * unit
        ds = (p * (dp_ref[slab, cols].astype(jnp.float32) - t_ref[h : h + 1, q0:tok])).astype(jnp.bfloat16)
        dv = dv + dot(p.astype(jnp.bfloat16), g_ref[q0:tok, lanes], NN)
        dk = dk + dot(ds, q_ref[q0:tok, lanes], NN)
        dq_ref[h, :, q0:tok] += dot(keys, ds, TN)
    return dk * scale, dv


def kernel(tok, heads, dim, q_ref, g_ref, kv_ref, ends_ref, dq_out, term_ref, e_ref, dp_ref, m_ref, l_ref, t_ref, mc_ref, dq_ref):
    scale = 1.0 / math.sqrt(dim)
    slope = scale * math.log2(math.e)
    chunks = tok // CHUNK
    sizes = (tok, heads, dim, slope)

    def stats(d, r, q0=0, first=False):
        stats_step(d, r, q0, first, *sizes, q_ref, g_ref, kv_ref, ends_ref, e_ref, dp_ref, m_ref, l_ref, t_ref, mc_ref)

    def grads(d, r, q0=0):
        dk, dv = grads_step(d, r, q0, *sizes, scale, q_ref, g_ref, kv_ref, e_ref, dp_ref, m_ref, l_ref, t_ref, mc_ref, dq_ref)
        rows = pl.ds(r * CHUNK, CHUNK) if isinstance(r, int) else pl.ds(pl.multiple_of(r * CHUNK, CHUNK), CHUNK)
        term_ref[d, rows, 0:dim] = dk.astype(jnp.bfloat16)
        term_ref[d, rows, dim : 2 * dim] = dv.astype(jnp.bfloat16)

    for r in range(chunks):
        stats(0, r, r * CHUNK, r == 0)

    for d in range(1, WINDOW + 1):

        @pl.loop(0, chunks)
        def _(r, d=d):
            stats(d, r)

    inv = 1.0 / l_ref[...]
    l_ref[...] = inv
    t_ref[...] = t_ref[...] * inv
    dq_ref[...] = jnp.zeros_like(dq_ref)
    for d in (4, 3, 2, 1):

        @pl.loop(0, chunks)
        def _(r, d=d):
            grads(d, r)

    for r in range(chunks):
        grads(0, r, r * CHUNK)
    for h in range(heads):
        dq_out[:, h * dim : (h + 1) * dim] = (dq_ref[h] * scale).T.astype(jnp.bfloat16)


def passed_along(shard, axis, by):
    count = lax.axis_size(axis)
    pairs = [(i, i + by) for i in range(count) if 0 <= i + by < count]
    return lax.ppermute(shard, axis, pairs)


def body(query_rows, key_rows, value_rows, grad_out, subtree_end):
    tok, dim = key_rows.shape
    heads = query_rows.shape[1] // dim
    kv = jnp.concatenate([key_rows, value_rows], axis=1)
    ends = subtree_end.reshape(tok // 128, 128)
    kvs = [kv] + [passed_along(kv, "blk", d) for d in range(1, WINDOW + 1)]
    end_list = [ends] + [passed_along(ends, "blk", d) for d in range(1, WINDOW + 1)]
    window = WINDOW + 1
    chunks = tok // CHUNK
    dq, terms = pl.pallas_call(
        functools.partial(kernel, tok, heads, dim),
        out_shape=(
            jax.ShapeDtypeStruct((tok, heads * dim), jnp.bfloat16),
            jax.ShapeDtypeStruct((window, tok, 2 * dim), jnp.bfloat16),
        ),
        in_specs=[pl.BlockSpec(memory_space=pltpu.VMEM)] * 4,
        out_specs=[pl.BlockSpec(memory_space=pltpu.VMEM)] * 2,
        scratch_shapes=[
            pltpu.VMEM((window * tok, heads * tok), jnp.bfloat16),
            pltpu.VMEM((window * tok, heads * tok), jnp.bfloat16),
            pltpu.VMEM((heads, tok), jnp.float32),
            pltpu.VMEM((heads, tok), jnp.float32),
            pltpu.VMEM((heads, tok), jnp.float32),
            pltpu.VMEM((window * chunks, heads, tok), jnp.float32),
            pltpu.VMEM((heads, dim, tok), jnp.float32),
        ],
        compiler_params=pltpu.CompilerParams(vmem_limit_bytes=48 * 2**20),
    )(query_rows, grad_out, jnp.stack(kvs), jnp.stack(end_list))
    total = terms[0].astype(jnp.float32)
    for d in range(1, window):
        total = total + passed_along(terms[d], "blk", -d).astype(jnp.float32)
    half = lax.psum_scatter(total.astype(jnp.bfloat16), "head", scatter_dimension=0, tiled=True)
    return dq, half[:, :dim], half[:, dim:]


def solution(mesh):
    placed = (P("blk", "head"), P("blk", None), P("blk", None), P("blk", "head"), P("blk"))
    return jax.shard_map(
        body,
        mesh=mesh,
        in_specs=placed,
        out_specs=(P("blk", "head"), P(("blk", "head"), None), P(("blk", "head"), None)),
        check_vma=False,
    )
```

profile of v0, /device:TPU:0, one launch (start us, length us, event | category | flops | bytes accessed | tf_op | source)
XLA Modules:
  0.0 118.6 jit_solution(14288095096961341269)
XLA Ops:
  7.2 0.0 reduce-scatter.2.cloned.1.call-start
  7.2 0.9 constant_dynamic-update-slice_fusion.1
  8.1 0.9 constant_dynamic-update-slice_fusion
  9.1 2.4 %collective-permute-start = (bf16[512,256]{1,0:T(8,128)(2,1)S(1)}, bf16[512,256]{1,0:T(8,128)(2,1)S(1)}, u32[]{:S(2)}, u32[]{:S(2)}) collective-permute-start(bf16[512,256]{1,0:T(8,128)(2,1)S(1)} %constant_dynamic-update-slice_fusion), channel_id=1, source_target_pairs={{0,2},{2,4},{4,6},{6,8},{8,10},{10,12},{12,14},{14,16},{16,18},{18... | collective-permute-start | bytes 786440 | tf_op jit(solution)/shard_map/ppermute | solution.py:139
  11.5 4.4 %collective-permute-start.1 = (bf16[512,256]{1,0:T(8,128)(2,1)S(1)}, bf16[512,256]{1,0:T(8,128)(2,1)S(1)}, u32[]{:S(2)}, u32[]{:S(2)}) collective-permute-start(bf16[512,256]{1,0:T(8,128)(2,1)S(1)} %constant_dynamic-update-slice_fusion), channel_id=1, source_target_pairs={{0,4},{2,6},{4,8},{6,10},{8,12},{10,14},{12,16},{14,18},{16,20},{1... | collective-permute-start | bytes 786440 | tf_op jit(solution)/shard_map/ppermute | solution.py:139
  15.9 4.4 %collective-permute-start.2 = (bf16[512,256]{1,0:T(8,128)(2,1)S(1)}, bf16[512,256]{1,0:T(8,128)(2,1)S(1)}, u32[]{:S(2)}, u32[]{:S(2)}) collective-permute-start(bf16[512,256]{1,0:T(8,128)(2,1)S(1)} %constant_dynamic-update-slice_fusion), channel_id=1, source_target_pairs={{0,6},{2,8},{4,10},{6,12},{8,14},{10,16},{12,18},{14,20},{16,22},{... | collective-permute-start | bytes 786440 | tf_op jit(solution)/shard_map/ppermute | solution.py:139
  20.3 3.5 %collective-permute-start.3 = (bf16[512,256]{1,0:T(8,128)(2,1)S(1)}, bf16[512,256]{1,0:T(8,128)(2,1)S(1)}, u32[]{:S(2)}, u32[]{:S(2)}) collective-permute-start(bf16[512,256]{1,0:T(8,128)(2,1)S(1)} %constant_dynamic-update-slice_fusion), channel_id=1, source_target_pairs={{0,8},{2,10},{4,12},{6,14},{8,16},{10,18},{12,20},{14,22},{16,24},... | collective-permute-start | bytes 786440 | tf_op jit(solution)/shard_map/ppermute | solution.py:139
  23.8 0.0 copy-start
  23.8 0.0 copy-start.1
  23.8 1.4 %collective-permute-start.4 = (s32[4,128]{1,0:T(4,128)}, s32[4,128]{1,0:T(4,128)S(1)}, u32[]{:S(2)}, u32[]{:S(2)}) collective-permute-start(s32[4,128]{1,0:T(4,128)} %bitcast.32), channel_id=1, source_target_pairs={{0,2},{2,4},{4,6},{6,8},{8,10},{10,12},{12,14},{14,16},{16,18},{18... | collective-permute-start | bytes 6152 | tf_op jit(solution)/shard_map/ppermute | solution.py:139
  25.2 0.7 constant_dynamic-update-slice_fusion.6
  25.9 0.3 collective-permute-done.4
  26.2 6.2 %collective-permute-start.5 = (s32[4,128]{1,0:T(4,128)}, s32[4,128]{1,0:T(4,128)S(1)}, u32[]{:S(2)}, u32[]{:S(2)}) collective-permute-start(s32[4,128]{1,0:T(4,128)} %bitcast.33), channel_id=1, source_target_pairs={{0,4},{2,6},{4,8},{6,10},{8,12},{10,14},{12,16},{14,18},{16,20},{1... | collective-permute-start | bytes 6152 | tf_op jit(solution)/shard_map/ppermute | solution.py:139
  32.5 1.5 %collective-permute-done.5 = s32[4,128]{1,0:T(4,128)S(1)} collective-permute-done((s32[4,128]{1,0:T(4,128)}, s32[4,128]{1,0:T(4,128)S(1)}, u32[]{:S(2)}, u32[]{:S(2)}) %collective-permute-start.5) | collective-permute-done | bytes 2080 | tf_op jit(solution)/shard_map/ppermute | solution.py:139
  34.0 7.8 %collective-permute-start.6 = (s32[4,128]{1,0:T(4,128)}, s32[4,128]{1,0:T(4,128)S(1)}, u32[]{:S(2)}, u32[]{:S(2)}) collective-permute-start(s32[4,128]{1,0:T(4,128)} %bitcast.34), channel_id=1, source_target_pairs={{0,6},{2,8},{4,10},{6,12},{8,14},{10,16},{12,18},{14,20},{16,22},{... | collective-permute-start | bytes 6152 | tf_op jit(solution)/shard_map/ppermute | solution.py:139
  41.8 1.5 %collective-permute-done.6 = s32[4,128]{1,0:T(4,128)S(1)} collective-permute-done((s32[4,128]{1,0:T(4,128)}, s32[4,128]{1,0:T(4,128)S(1)}, u32[]{:S(2)}, u32[]{:S(2)}) %collective-permute-start.6) | collective-permute-done | bytes 2080 | tf_op jit(solution)/shard_map/ppermute | solution.py:139
  43.3 7.8 %collective-permute-start.7 = (s32[4,128]{1,0:T(4,128)}, s32[4,128]{1,0:T(4,128)S(1)}, u32[]{:S(2)}, u32[]{:S(2)}) collective-permute-start(s32[4,128]{1,0:T(4,128)} %bitcast.35), channel_id=1, source_target_pairs={{0,8},{2,10},{4,12},{6,14},{8,16},{10,18},{12,20},{14,22},{16,24},... | collective-permute-start | bytes 6152 | tf_op jit(solution)/shard_map/ppermute | solution.py:139
  51.2 1.5 %collective-permute-done.7 = s32[4,128]{1,0:T(4,128)S(1)} collective-permute-done((s32[4,128]{1,0:T(4,128)}, s32[4,128]{1,0:T(4,128)S(1)}, u32[]{:S(2)}, u32[]{:S(2)}) %collective-permute-start.7) | collective-permute-done | bytes 2080 | tf_op jit(solution)/shard_map/ppermute | solution.py:139
  52.7 0.0 collective-permute-done
  52.7 0.0 collective-permute-done.1
  52.7 0.0 collective-permute-done.2
  52.8 0.0 collective-permute-done.3
  52.8 0.0 copy-done
  52.8 0.0 copy-done.1
  52.8 19.8 %shard_map.76 = (bf16[512,512]{1,0:T(8,128)(2,1)}, bf16[5,512,256]{2,1,0:T(8,128)(2,1)S(1)}) custom-call(bf16[512,512]{1,0:T(8,128)(2,1)S(1)} %copy-done, bf16[512,512]{1,0:T(8,128)(2,1)S(1)} %copy-done.1, bf16[5,512,256]{2,1,0:T(8,128)(2,1)S(1)} %bitcast_dynamic-update-slice_fusion.kv_ref, s32[5,4,128]{2,1,0:T(4,128)S(1)} %constant_dynamic-update-slice_fusion.2.ends_ref), custom_call_target="tpu_custom_call" | custom-call | tf_op jit(solution)/shard_map/pallas_call | solution.py:151
  72.6 0.1 slice_bitcast_fusion.3
  72.7 1.3 %collective-permute-start.10 = (bf16[512,256]{1,0:T(8,128)(2,1)S(1)}, bf16[512,256]{1,0:T(8,128)(2,1)S(1)}, u32[]{:S(2)}, u32[]{:S(2)}) collective-permute-start(bf16[512,256]{1,0:T(8,128)(2,1)S(1)} %get-tuple-element.9), channel_id=1, source_target_pairs={{6,0},{8,2},{10,4},{12,6},{14,8},{16,10},{18,12},{20,14},{22,16},{... | collective-permute-start | bytes 786440 | tf_op jit(solution)/shard_map/ppermute | solution.py:139
  74.0 1.3 %collective-permute-start.11 = (bf16[512,256]{1,0:T(8,128)(2,1)S(1)}, bf16[512,256]{1,0:T(8,128)(2,1)S(1)}, u32[]{:S(2)}, u32[]{:S(2)}) collective-permute-start(bf16[512,256]{1,0:T(8,128)(2,1)S(1)} %get-tuple-element.8), channel_id=1, source_target_pairs={{8,0},{10,2},{12,4},{14,6},{16,8},{18,10},{20,12},{22,14},{24,16},... | collective-permute-start | bytes 786440 | tf_op jit(solution)/shard_map/ppermute | solution.py:139
  75.3 1.3 %collective-permute-start.8 = (bf16[512,256]{1,0:T(8,128)(2,1)S(1)}, bf16[512,256]{1,0:T(8,128)(2,1)S(1)}, u32[]{:S(2)}, u32[]{:S(2)}) collective-permute-start(bf16[512,256]{1,0:T(8,128)(2,1)S(1)} %get-tuple-element.7), channel_id=1, source_target_pairs={{2,0},{4,2},{6,4},{8,6},{10,8},{12,10},{14,12},{16,14},{18,16},{20... | collective-permute-start | bytes 786440 | tf_op jit(solution)/shard_map/ppermute | solution.py:139
  76.6 1.3 %collective-permute-start.9 = (bf16[512,256]{1,0:T(8,128)(2,1)S(1)}, bf16[512,256]{1,0:T(8,128)(2,1)S(1)}, u32[]{:S(2)}, u32[]{:S(2)}) collective-permute-start(bf16[512,256]{1,0:T(8,128)(2,1)S(1)} %get-tuple-element.10), channel_id=1, source_target_pairs={{4,0},{6,2},{8,4},{10,6},{12,8},{14,10},{16,12},{18,14},{20,16},{2... | collective-permute-start | bytes 786440 | tf_op jit(solution)/shard_map/ppermute | solution.py:139
  77.9 3.9 %collective-permute-done.10 = bf16[512,256]{1,0:T(8,128)(2,1)S(1)} collective-permute-done((bf16[512,256]{1,0:T(8,128)(2,1)S(1)}, bf16[512,256]{1,0:T(8,128)(2,1)S(1)}, u32[]{:S(2)}, u32[]{:S(2)}) %collective-permute-start.10) | collective-permute-done | bytes 262176 | tf_op jit(solution)/shard_map/ppermute | solution.py:139
  81.8 7.9 %collective-permute-done.11 = bf16[512,256]{1,0:T(8,128)(2,1)S(1)} collective-permute-done((bf16[512,256]{1,0:T(8,128)(2,1)S(1)}, bf16[512,256]{1,0:T(8,128)(2,1)S(1)}, u32[]{:S(2)}, u32[]{:S(2)}) %collective-permute-start.11) | collective-permute-done | bytes 262176 | tf_op jit(solution)/shard_map/ppermute | solution.py:139
  89.7 0.0 collective-permute-done.8
  89.7 0.0 collective-permute-done.9
  89.7 0.9 fusion.3
  90.6 0.0 reduce-scatter.2.cloned.1.call-update
  90.6 19.5 %reduce-scatter.2.cloned.1.call-done = bf16[256,256]{1,0:T(8,128)(2,1)} async-done(((bf16[512,256]{1,0:T(8,128)(2,1)}), bf16[256,256]{1,0:T(8,128)(2,1)}) %reduce-scatter.2.cloned.1.call-update) | async-done | bytes 131088 | tf_op jit(solution)/shard_map/reduce_scatter | solution.py:173
  110.2 1.5 %fusion.4 = (bf16[256,128]{1,0:T(8,128)(2,1)}, bf16[256,128]{1,0:T(8,128)(2,1)}) fusion(bf16[256,256]{1,0:T(8,128)(2,1)} %reduce-scatter.2.cloned.1.call-done), kind=kLoop, calls=%fused_computation.21 | loop fusion | bytes 262144 | tf_op jit(solution)/shard_map/slice | solution.py:174
  (9 shorter events, 0.1 us)
Async XLA Ops:
  7.2 103.0 %reduce-scatter.2.cloned.1.call-start = ((), (), s32[]{:S(2)}) async-start(), calls=%async_computation.1 | async-start | bytes 393216 | tf_op jit(solution)/shard_map/reduce_scatter | solution.py:173
  9.1 43.6 %collective-permute-start = (bf16[512,256]{1,0:T(8,128)(2,1)S(1)}, bf16[512,256]{1,0:T(8,128)(2,1)S(1)}, u32[]{:S(2)}, u32[]{:S(2)}) collective-permute-start(bf16[512,256]{1,0:T(8,128)(2,1)S(1)} %constant_dynamic-update-slice_fusion), channel_id=1, source_target_pairs={{0,2},{2,4},{4,6},{6,8},{8,10},{10,12},{12,14},{14,16},{16,18},{18... | collective-permute-start | bytes 786440 | tf_op jit(solution)/shard_map/ppermute | solution.py:139
  11.5 41.2 %collective-permute-start.1 = (bf16[512,256]{1,0:T(8,128)(2,1)S(1)}, bf16[512,256]{1,0:T(8,128)(2,1)S(1)}, u32[]{:S(2)}, u32[]{:S(2)}) collective-permute-start(bf16[512,256]{1,0:T(8,128)(2,1)S(1)} %constant_dynamic-update-slice_fusion), channel_id=1, source_target_pairs={{0,4},{2,6},{4,8},{6,10},{8,12},{10,14},{12,16},{14,18},{16,20},{1... | collective-permute-start | bytes 786440 | tf_op jit(solution)/shard_map/ppermute | solution.py:139
  15.9 36.9 %collective-permute-start.2 = (bf16[512,256]{1,0:T(8,128)(2,1)S(1)}, bf16[512,256]{1,0:T(8,128)(2,1)S(1)}, u32[]{:S(2)}, u32[]{:S(2)}) collective-permute-start(bf16[512,256]{1,0:T(8,128)(2,1)S(1)} %constant_dynamic-update-slice_fusion), channel_id=1, source_target_pairs={{0,6},{2,8},{4,10},{6,12},{8,14},{10,16},{12,18},{14,20},{16,22},{... | collective-permute-start | bytes 786440 | tf_op jit(solution)/shard_map/ppermute | solution.py:139
  20.3 32.5 %collective-permute-start.3 = (bf16[512,256]{1,0:T(8,128)(2,1)S(1)}, bf16[512,256]{1,0:T(8,128)(2,1)S(1)}, u32[]{:S(2)}, u32[]{:S(2)}) collective-permute-start(bf16[512,256]{1,0:T(8,128)(2,1)S(1)} %constant_dynamic-update-slice_fusion), channel_id=1, source_target_pairs={{0,8},{2,10},{4,12},{6,14},{8,16},{10,18},{12,20},{14,22},{16,24},... | collective-permute-start | bytes 786440 | tf_op jit(solution)/shard_map/ppermute | solution.py:139
  23.8 29.1 %copy-start = (bf16[512,512]{1,0:T(8,128)(2,1)S(1)}, bf16[512,512]{1,0:T(8,128)(2,1)}, u32[]{:S(2)}) copy-start(bf16[512,512]{1,0:T(8,128)(2,1)} %q_ref.1) | copy-start | bytes 1572868
  23.8 29.1 %copy-start.1 = (bf16[512,512]{1,0:T(8,128)(2,1)S(1)}, bf16[512,512]{1,0:T(8,128)(2,1)}, u32[]{:S(2)}) copy-start(bf16[512,512]{1,0:T(8,128)(2,1)} %g_ref.1) | copy-start | bytes 1572868
  23.8 2.4 %collective-permute-start.4 = (s32[4,128]{1,0:T(4,128)}, s32[4,128]{1,0:T(4,128)S(1)}, u32[]{:S(2)}, u32[]{:S(2)}) collective-permute-start(s32[4,128]{1,0:T(4,128)} %bitcast.32), channel_id=1, source_target_pairs={{0,2},{2,4},{4,6},{6,8},{8,10},{10,12},{12,14},{14,16},{16,18},{18... | collective-permute-start | bytes 6152 | tf_op jit(solution)/shard_map/ppermute | solution.py:139
  26.2 7.8 %collective-permute-start.5 = (s32[4,128]{1,0:T(4,128)}, s32[4,128]{1,0:T(4,128)S(1)}, u32[]{:S(2)}, u32[]{:S(2)}) collective-permute-start(s32[4,128]{1,0:T(4,128)} %bitcast.33), channel_id=1, source_target_pairs={{0,4},{2,6},{4,8},{6,10},{8,12},{10,14},{12,16},{14,18},{16,20},{1... | collective-permute-start | bytes 6152 | tf_op jit(solution)/shard_map/ppermute | solution.py:139
  34.0 9.3 %collective-permute-start.6 = (s32[4,128]{1,0:T(4,128)}, s32[4,128]{1,0:T(4,128)S(1)}, u32[]{:S(2)}, u32[]{:S(2)}) collective-permute-start(s32[4,128]{1,0:T(4,128)} %bitcast.34), channel_id=1, source_target_pairs={{0,6},{2,8},{4,10},{6,12},{8,14},{10,16},{12,18},{14,20},{16,22},{... | collective-permute-start | bytes 6152 | tf_op jit(solution)/shard_map/ppermute | solution.py:139
  43.3 9.4 %collective-permute-start.7 = (s32[4,128]{1,0:T(4,128)}, s32[4,128]{1,0:T(4,128)S(1)}, u32[]{:S(2)}, u32[]{:S(2)}) collective-permute-start(s32[4,128]{1,0:T(4,128)} %bitcast.35), channel_id=1, source_target_pairs={{0,8},{2,10},{4,12},{6,14},{8,16},{10,18},{12,20},{14,22},{16,24},... | collective-permute-start | bytes 6152 | tf_op jit(solution)/shard_map/ppermute | solution.py:139
  72.7 9.1 %collective-permute-start.10 = (bf16[512,256]{1,0:T(8,128)(2,1)S(1)}, bf16[512,256]{1,0:T(8,128)(2,1)S(1)}, u32[]{:S(2)}, u32[]{:S(2)}) collective-permute-start(bf16[512,256]{1,0:T(8,128)(2,1)S(1)} %get-tuple-element.9), channel_id=1, source_target_pairs={{6,0},{8,2},{10,4},{12,6},{14,8},{16,10},{18,12},{20,14},{22,16},{... | collective-permute-start | bytes 786440 | tf_op jit(solution)/shard_map/ppermute | solution.py:139
  74.0 15.7 %collective-permute-start.11 = (bf16[512,256]{1,0:T(8,128)(2,1)S(1)}, bf16[512,256]{1,0:T(8,128)(2,1)S(1)}, u32[]{:S(2)}, u32[]{:S(2)}) collective-permute-start(bf16[512,256]{1,0:T(8,128)(2,1)S(1)} %get-tuple-element.8), channel_id=1, source_target_pairs={{8,0},{10,2},{12,4},{14,6},{16,8},{18,10},{20,12},{22,14},{24,16},... | collective-permute-start | bytes 786440 | tf_op jit(solution)/shard_map/ppermute | solution.py:139
  75.3 14.4 %collective-permute-start.8 = (bf16[512,256]{1,0:T(8,128)(2,1)S(1)}, bf16[512,256]{1,0:T(8,128)(2,1)S(1)}, u32[]{:S(2)}, u32[]{:S(2)}) collective-permute-start(bf16[512,256]{1,0:T(8,128)(2,1)S(1)} %get-tuple-element.7), channel_id=1, source_target_pairs={{2,0},{4,2},{6,4},{8,6},{10,8},{12,10},{14,12},{16,14},{18,16},{20... | collective-permute-start | bytes 786440 | tf_op jit(solution)/shard_map/ppermute | solution.py:139
  76.6 13.1 %collective-permute-start.9 = (bf16[512,256]{1,0:T(8,128)(2,1)S(1)}, bf16[512,256]{1,0:T(8,128)(2,1)S(1)}, u32[]{:S(2)}, u32[]{:S(2)}) collective-permute-start(bf16[512,256]{1,0:T(8,128)(2,1)S(1)} %get-tuple-element.10), channel_id=1, source_target_pairs={{4,0},{6,2},{8,4},{10,6},{12,8},{14,10},{16,12},{18,14},{20,16},{2... | collective-permute-start | bytes 786440 | tf_op jit(solution)/shard_map/ppermute | solution.py:139
Sparse Core Ops, SparseCore 0:
  90.8 19.3 reduce-scatter.1
where the time goes:
time: 119 us
  starting transfers between devices  43.2 us (36%)
  waiting for transfers between devices  36.2 us (30%)
  Pallas kernels  19.8 us (17%)
  between operations  14.2 us (12%)
  local copies, waits for them, and re-layouts  4.29 us (4%)
    ppermute x12, starting transfers between devices, passed_along(): return lax.ppermute(shard, axis, pairs)  43.1 us
    pallas_call x1, Pallas kernels, body(): pl.pallas_call(functools.partial(kernel, tok, heads, dim), out_shape=(jax...  19.8 us
    reduce_scatter x1, waiting for transfers between devices, body(): lax.psum_scatter(total.astype(jnp.bfloat16), 'head', scatter_dimension=0,...  19.5 us
    ppermute x12, waiting for transfers between devices, passed_along(): return lax.ppermute(shard, axis, pairs)  16.6 us
  transfers between devices with their start and end apart: 13, of which 7 were waited for; matrix products, arithmetic and copies ran while one was open for 1% of the time, Pallas kernels for 0%

commit v1 on v0

--- a/solution.py
+++ b/solution.py
@@ -93,11 +93,61 @@
     return dk * scale, dv
 
 
-def kernel(tok, heads, dim, q_ref, g_ref, kv_ref, ends_ref, dq_out, term_ref, e_ref, dp_ref, m_ref, l_ref, t_ref, mc_ref, dq_ref):
+def kernel(tok, heads, dim, q_ref, g_ref, k_ref, v_ref, own_ends_ref, dq_out, dk_out, dv_out, kv_ref, ends_ref, term_ref, sib_ref, yin_ref, home_ref, e_ref, dp_ref, m_ref, l_ref, t_ref, mc_ref, dq_ref, ends_sem, direct_sem, relay_sem, core_sem, sib_sem, swap_sem, home_sem):
     scale = 1.0 / math.sqrt(dim)
     slope = scale * math.log2(math.e)
     chunks = tok // CHUNK
     sizes = (tok, heads, dim, slope)
+    b = lax.axis_index("blk")
+    y = lax.axis_index("head")
+    count = lax.axis_size("blk")
+    core = lax.rem(b, 2)
+    sibling = b + 1 - 2 * core
+    mine = pl.ds(pl.multiple_of(y * CHUNK, CHUNK), CHUNK)
+    other = pl.ds(pl.multiple_of((1 - y) * CHUNK, CHUNK), CHUNK)
+
+    def at(shift):
+        return lax.rem(b + shift + count, count)
+
+    def remote(src, dst, sems, slot, to_b, to_y):
+        return pltpu.make_async_remote_copy(
+            src_ref=src, dst_ref=dst, send_sem=sems.at[0, slot], recv_sem=sems.at[1, slot],
+            device_id=(to_b, to_y), device_id_type=pl.DeviceIdType.MESH,
+        )
+
+    def ends_copy(d):
+        return remote(ends_ref.at[0], ends_ref.at[d], ends_sem, d, at(d), y)
+
+    def direct_copy(d):
+        return remote(kv_ref.at[0, mine], kv_ref.at[d, mine], direct_sem, d // 2, at(d), y)
+
+    def relay_copy(d):
+        return remote(kv_ref.at[d, mine], kv_ref.at[d, mine], relay_sem, d // 2, b, 1 - y)
+
+    def relay_arrival(d):
+        return remote(kv_ref.at[d, other], kv_ref.at[d, other], relay_sem, d // 2, b, 1 - y)
+
+    def core_copy(slot):
+        return remote(kv_ref.at[slot - 1 + 2 * core], kv_ref.at[slot], core_sem, slot, sibling, y)
+
+    def sib_copy(d):
+        return remote(term_ref.at[d], sib_ref.at[d // 2], sib_sem, d // 2, sibling, y)
+
+    def swap_copy(d):
+        return remote(term_ref.at[d, other], yin_ref.at[d // 2], swap_sem, d // 2, b, 1 - y)
+
+    def home_copy(d):
+        return remote(term_ref.at[d, mine], home_ref.at[d // 2 - 1], home_sem, d // 2 - 1, at(-d), y)
+
+    barrier = pltpu.get_barrier_semaphore()
+    for d in range(1, WINDOW + 1):
+        for shift in (d, -d):
+            pl.semaphore_signal(barrier, inc=1, device_id=(at(shift), y), device_id_type=pl.DeviceIdType.MESH)
+    pl.semaphore_signal(barrier, inc=1, device_id=(b, 1 - y), device_id_type=pl.DeviceIdType.MESH)
+    kv_ref[0, :, 0:dim] = k_ref[...]
+    kv_ref[0, :, dim : 2 * dim] = v_ref[...]
+    ends_ref[0] = own_ends_ref[...]
+    pl.semaphore_wait(barrier, 2 * WINDOW + 1)
 
     def stats(d, r, q0=0, first=False):
         stats_step(d, r, q0, first, *sizes, q_ref, g_ref, kv_ref, ends_ref, e_ref, dp_ref, m_ref, l_ref, t_ref, mc_ref)
@@ -108,55 +158,187 @@
         term_ref[d, rows, 0:dim] = dk.astype(jnp.bfloat16)
         term_ref[d, rows, dim : 2 * dim] = dv.astype(jnp.bfloat16)
 
-    for r in range(chunks):
-        stats(0, r, r * CHUNK, r == 0)
-
+    def all_stats(d):
+        @pl.loop(0, chunks)
+        def _(r):
+            stats(d, r)
+
+    for d in (2, 4):
+        direct_copy(d).start()
     for d in range(1, WINDOW + 1):
-
-        @pl.loop(0, chunks)
-        def _(r, d=d):
-            stats(d, r)
+        ends_copy(d).start()
+
+    @pl.when(core == 0)
+    def _():
+        core_copy(1).start()
+
+    stats(0, 0, 0, True)
+    direct_copy(2).wait_recv()
+    relay_copy(2).start()
+    stats(0, 1, CHUNK)
+    direct_copy(4).wait_recv()
+    relay_copy(4).start()
+    relay_arrival(2).wait_recv()
+
+    @pl.when(core == 0)
+    def _():
+        core_copy(3).start()
+
+    @pl.when(core == 1)
+    def _():
+        core_copy(1).start()
+
+    for d in range(1, WINDOW + 1):
+        ends_copy(d).wait_recv()
+    all_stats(2)
+    relay_arrival(4).wait_recv()
+
+    @pl.when(core == 1)
+    def _():
+        core_copy(3).start()
+
+    all_stats(4)
+    core_copy(1).wait_recv()
+    all_stats(1)
+    core_copy(3).wait_recv()
+    all_stats(3)
 
     inv = 1.0 / l_ref[...]
     l_ref[...] = inv
     t_ref[...] = t_ref[...] * inv
     dq_ref[...] = jnp.zeros_like(dq_ref)
-    for d in (4, 3, 2, 1):
+
+    def add(d, rows, part):
+        total = term_ref[d, rows, :].astype(jnp.float32) + part.astype(jnp.float32)
+        term_ref[d, rows, :] = total.astype(jnp.bfloat16)
+
+    def send_home(d):
+        swap_copy(d).wait_recv()
+        add(d, mine, yin_ref[d // 2])
+        home_copy(d).start()
+
+    for d in (3, 1):
 
         @pl.loop(0, chunks)
         def _(r, d=d):
             grads(d, r)
 
-    for r in range(chunks):
-        grads(0, r, r * CHUNK)
+        sib_copy(d).start()
+
+    @pl.loop(0, chunks)
+    def _(i):
+        r = lax.rem(1 - y + i, 2)
+        grads(4, r)
+        rows = pl.ds(pl.multiple_of(r * CHUNK, CHUNK), CHUNK)
+
+        @pl.when(core == 1)
+        def _():
+            @pl.when(i == 0)
+            def _():
+                sib_copy(3).wait_recv()
+
+            add(4, rows, sib_ref[1, rows, :])
+
+        @pl.when(i == 0)
+        def _():
+            swap_copy(4).start()
+
+    @pl.loop(0, chunks)
+    def _(i):
+        r = lax.rem(1 - y + i, 2)
+        grads(2, r)
+        rows = pl.ds(pl.multiple_of(r * CHUNK, CHUNK), CHUNK)
+
+        @pl.when(i == 0)
+        def _():
+            @pl.when(core == 1)
+            def _():
+                sib_copy(1).wait_recv()
+
+            @pl.when(core == 0)
+            def _():
+                sib_copy(3).wait_recv()
+
+        add(2, rows, sib_ref[1 - core, rows, :])
+
+        @pl.when(i == 0)
+        def _():
+            swap_copy(2).start()
+            send_home(4)
+
+    @pl.when(y == 0)
+    def _():
+        grads(0, 1, CHUNK)
+
+    @pl.when(y == 1)
+    def _():
+        grads(0, 0)
+
+    @pl.when(core == 0)
+    def _():
+        sib_copy(1).wait_recv()
+        add(0, other, sib_ref[0, other, :])
+
+    swap_copy(0).start()
+    send_home(2)
+
+    @pl.when(y == 0)
+    def _():
+        grads(0, 0)
+
+    @pl.when(y == 1)
+    def _():
+        grads(0, 1, CHUNK)
+
+    @pl.when(core == 0)
+    def _():
+        add(0, mine, sib_ref[0, mine, :])
+
     for h in range(heads):
         dq_out[:, h * dim : (h + 1) * dim] = (dq_ref[h] * scale).T.astype(jnp.bfloat16)
-
-
-def passed_along(shard, axis, by):
-    count = lax.axis_size(axis)
-    pairs = [(i, i + by) for i in range(count) if 0 <= i + by < count]
-    return lax.ppermute(shard, axis, pairs)
+    total = term_ref[0, mine, :].astype(jnp.float32)
+    for d in (2, 4):
+        home_copy(d).wait_recv()
+        total = total + home_ref[d // 2 - 1].astype(jnp.float32)
+    swap_copy(0).wait_recv()
+    total = (total + yin_ref[0].astype(jnp.float32)).astype(jnp.bfloat16)
+    dk_out[...] = total[:, 0:dim]
+    dv_out[...] = total[:, dim : 2 * dim]
+    for d in range(1, WINDOW + 1):
+        ends_copy(d).wait_send()
+    for d in (2, 4):
+        direct_copy(d).wait_send()
+        relay_copy(d).wait_send()
+        home_copy(d).wait_send()
+    for d in (1, 3):
+        core_copy(d).wait_send()
+        sib_copy(d).wait_send()
+    for d in (0, 2, 4):
+        swap_copy(d).wait_send()
 
 
 def body(query_rows, key_rows, value_rows, grad_out, subtree_end):
     tok, dim = key_rows.shape
     heads = query_rows.shape[1] // dim
-    kv = jnp.concatenate([key_rows, value_rows], axis=1)
     ends = subtree_end.reshape(tok // 128, 128)
-    kvs = [kv] + [passed_along(kv, "blk", d) for d in range(1, WINDOW + 1)]
-    end_list = [ends] + [passed_along(ends, "blk", d) for d in range(1, WINDOW + 1)]
     window = WINDOW + 1
     chunks = tok // CHUNK
-    dq, terms = pl.pallas_call(
+    return pl.pallas_call(
         functools.partial(kernel, tok, heads, dim),
         out_shape=(
             jax.ShapeDtypeStruct((tok, heads * dim), jnp.bfloat16),
-            jax.ShapeDtypeStruct((window, tok, 2 * dim), jnp.bfloat16),
+            jax.ShapeDtypeStruct((CHUNK, dim), jnp.bfloat16),
+            jax.ShapeDtypeStruct((CHUNK, dim), jnp.bfloat16),
         ),
-        in_specs=[pl.BlockSpec(memory_space=pltpu.VMEM)] * 4,
-        out_specs=[pl.BlockSpec(memory_space=pltpu.VMEM)] * 2,
+        in_specs=[pl.BlockSpec(memory_space=pltpu.VMEM)] * 5,
+        out_specs=[pl.BlockSpec(memory_space=pltpu.VMEM)] * 3,
         scratch_shapes=[
+            pltpu.VMEM((window, tok, 2 * dim), jnp.bfloat16),
+            pltpu.VMEM((window, tok // 128, 128), jnp.int32),
+            pltpu.VMEM((window, tok, 2 * dim), jnp.bfloat16),
+            pltpu.VMEM((2, tok, 2 * dim), jnp.bfloat16),
+            pltpu.VMEM((3, CHUNK, 2 * dim), jnp.bfloat16),
+            pltpu.VMEM((2, CHUNK, 2 * dim), jnp.bfloat16),
             pltpu.VMEM((window * tok, heads * tok), jnp.bfloat16),
             pltpu.VMEM((window * tok, heads * tok), jnp.bfloat16),
             pltpu.VMEM((heads, tok), jnp.float32),
@@ -164,14 +346,18 @@
             pltpu.VMEM((heads, tok), jnp.float32),
             pltpu.VMEM((window * chunks, heads, tok), jnp.float32),
             pltpu.VMEM((heads, dim, tok), jnp.float32),
+            pltpu.SemaphoreType.DMA((2, window)),
+            pltpu.SemaphoreType.DMA((2, 3)),
+            pltpu.SemaphoreType.DMA((2, 3)),
+            pltpu.SemaphoreType.DMA((2, 4)),
+            pltpu.SemaphoreType.DMA((2, 2)),
+            pltpu.SemaphoreType.DMA((2, 3)),
+            pltpu.SemaphoreType.DMA((2, 2)),
         ],
-        compiler_params=pltpu.CompilerParams(vmem_limit_bytes=48 * 2**20),
-    )(query_rows, grad_out, jnp.stack(kvs), jnp.stack(end_list))
-    total = terms[0].astype(jnp.float32)
-    for d in range(1, window):
-        total = total + passed_along(terms[d], "blk", -d).astype(jnp.float32)
-    half = lax.psum_scatter(total.astype(jnp.bfloat16), "head", scatter_dimension=0, tiled=True)
-    return dq, half[:, :dim], half[:, dim:]
+        compiler_params=pltpu.CompilerParams(
+            vmem_limit_bytes=48 * 2**20, collective_id=0, has_side_effects=True
+        ),
+    )(query_rows, grad_out, key_rows, value_rows, ends)
 
 
 def solution(mesh):

time: 119 us -> 49.5 us (0.42)
  starting transfers between devices: 43.2 us -> 0 us
  waiting for transfers between devices: 36.2 us -> 0 us
  Pallas kernels: 19.8 us -> 42 us
  between operations: 14.2 us -> 0.65 us
  local copies, waits for them, and re-layouts: 4.29 us -> 6.62 us
    ppermute x12 -> x0, starting transfers between devices: 43.1 us -> none  [passed_along(): return lax.ppermute(shard, axis, pairs)]
    pallas_call x1, Pallas kernels: 19.8 us -> 42 us  [body(): pl.pallas_call(functools.partial(kernel, tok, heads, dim), out_shape=(jax...]
    reduce_scatter x1 -> x0, waiting for transfers between devices: 19.5 us -> none  [body(): lax.psum_scatter(total.astype(jnp.bfloat16), 'head', scatter_dimension=0,...]
    ppermute x12 -> x0, waiting for transfers between devices: 16.6 us -> none  [passed_along(): return lax.ppermute(shard, axis, pairs)]
    unnamed x13, local copies, waits for them, and re-layouts: 1.73 us -> 6.62 us
    slice x1 -> x0, local copies, waits for them, and re-layouts: 1.53 us -> none  [body(): return (dq, half[:, :dim], half[:, dim:])]
  transfers between devices with their start and end apart: 13 -> 0, of which waited for: 7 -> 0; matrix products, arithmetic and copies ran while one was open for 1% -> 0% of each run, Pallas kernels for 0% -> 0%
where the time goes in v1:
time: 49.5 us; the launch traced here: 49.3 us
  Pallas kernels  42 us (85%)
  local copies, waits for them, and re-layouts  6.62 us (13%)
  between operations  0.65 us (1%)
    pallas_call x1, Pallas kernels, body(): pl.pallas_call(functools.partial(kernel, tok, heads, dim), out_shape=(jax...  42 us
    unnamed x13, local copies, waits for them, and re-layouts  6.62 us

profile of v1, /device:TPU:0, one launch (start us, length us, event | category | flops | bytes accessed | tf_op | source)
XLA Modules:
  0.0 49.3 jit_solution(1918625827036318405)
XLA Ops:
  0.6 0.0 copy-start
  0.6 1.0 %copy-done = bf16[512,512]{1,0:T(8,128)(2,1)S(1)} copy-done((bf16[512,512]{1,0:T(8,128)(2,1)S(1)}, bf16[512,512]{1,0:T(8,128)(2,1)}, u32[]{:S(2)}) %copy-start) | copy-done | bytes 524312
  1.7 0.0 copy-start.1
  1.7 1.0 %copy-done.1 = bf16[512,512]{1,0:T(8,128)(2,1)S(1)} copy-done((bf16[512,512]{1,0:T(8,128)(2,1)S(1)}, bf16[512,512]{1,0:T(8,128)(2,1)}, u32[]{:S(2)}) %copy-start.1) | copy-done | bytes 524312
  2.7 0.0 copy-start.2
  2.7 0.9 %copy-done.2 = bf16[512,128]{1,0:T(8,128)(2,1)S(1)} copy-done((bf16[512,128]{1,0:T(8,128)(2,1)S(1)}, bf16[512,128]{1,0:T(8,128)(2,1)}, u32[]{:S(2)}) %copy-start.2) | copy-done | bytes 131096
  3.6 0.0 copy-start.3
  3.6 0.9 %copy-done.3 = bf16[512,128]{1,0:T(8,128)(2,1)S(1)} copy-done((bf16[512,128]{1,0:T(8,128)(2,1)S(1)}, bf16[512,128]{1,0:T(8,128)(2,1)}, u32[]{:S(2)}) %copy-start.3) | copy-done | bytes 131096
  4.5 0.0 copy-start.4
  4.5 0.7 %copy-done.4 = s32[512]{0:T(512)S(1)} copy-done((s32[512]{0:T(512)S(1)}, s32[512]{0:T(512)}, u32[]{:S(2)}) %copy-start.4) | copy-done | bytes 2072
  5.2 42.0 %shard_map.76 = (bf16[512,512]{1,0:T(8,128)(2,1)S(1)}, bf16[256,128]{1,0:T(8,128)(2,1)S(1)}, bf16[256,128]{1,0:T(8,128)(2,1)S(1)}) custom-call(bf16[512,512]{1,0:T(8,128)(2,1)S(1)} %copy-done, bf16[512,512]{1,0:T(8,128)(2,1)S(1)} %copy-done.1, bf16[512,128]{1,0:T(8,128)(2,1)S(1)} %copy-done.2, bf16[512,128]{1,0:T(8,128)(2,1)S(1)} %copy-done.3, ...), custom_call_target="tpu_custom_call" | custom-call | tf_op jit(solution)/shard_map/pallas_call | solution.py:326
  47.2 0.8 %copy.11 = bf16[512,512]{1,0:T(8,128)(2,1)} copy(bf16[512,512]{1,0:T(8,128)(2,1)S(1)} %get-tuple-element.6) | data formatting | bytes 1048576
  48.0 0.6 %copy.12 = bf16[256,128]{1,0:T(8,128)(2,1)} copy(bf16[256,128]{1,0:T(8,128)(2,1)S(1)} %get-tuple-element.7) | data formatting | bytes 131072
  48.6 0.6 %copy.13 = bf16[256,128]{1,0:T(8,128)(2,1)} copy(bf16[256,128]{1,0:T(8,128)(2,1)S(1)} %get-tuple-element.8) | data formatting | bytes 131072
Async XLA Ops:
  0.6 1.0 %copy-start = (bf16[512,512]{1,0:T(8,128)(2,1)S(1)}, bf16[512,512]{1,0:T(8,128)(2,1)}, u32[]{:S(2)}) copy-start(bf16[512,512]{1,0:T(8,128)(2,1)} %q_ref.1) | copy-start | bytes 1572868
  1.7 1.0 %copy-start.1 = (bf16[512,512]{1,0:T(8,128)(2,1)S(1)}, bf16[512,512]{1,0:T(8,128)(2,1)}, u32[]{:S(2)}) copy-start(bf16[512,512]{1,0:T(8,128)(2,1)} %g_ref.1) | copy-start | bytes 1572868
  2.7 0.9 %copy-start.2 = (bf16[512,128]{1,0:T(8,128)(2,1)S(1)}, bf16[512,128]{1,0:T(8,128)(2,1)}, u32[]{:S(2)}) copy-start(bf16[512,128]{1,0:T(8,128)(2,1)} %k_ref.1) | copy-start | bytes 393220
  3.6 0.9 %copy-start.3 = (bf16[512,128]{1,0:T(8,128)(2,1)S(1)}, bf16[512,128]{1,0:T(8,128)(2,1)}, u32[]{:S(2)}) copy-start(bf16[512,128]{1,0:T(8,128)(2,1)} %v_ref.1) | copy-start | bytes 393220
  4.5 0.7 %copy-start.4 = (s32[512]{0:T(512)S(1)}, s32[512]{0:T(512)}, u32[]{:S(2)}) copy-start(s32[512]{0:T(512)} %param.9) | copy-start | bytes 6148

commit v2 on v0

--- a/solution.py
+++ b/solution.py
@@ -35,7 +35,7 @@
         line = ends_ref[d, pl.ds(r * per + piece, 1), :]
         tiles.append(jnp.broadcast_to(line, (128, 128)).T)
     ends = jnp.concatenate(tiles, axis=0)
-    ends = jnp.where(blk >= d, ends - blk * tok, 0)
+    ends = ends - blk * tok
     spot = lax.broadcasted_iota(jnp.int32, (CHUNK, 128), 1) + q0
     key_spot = lax.broadcasted_iota(jnp.int32, (CHUNK, 128), 0) + (row0 - d * tok)
     bias = []
@@ -93,11 +93,82 @@
     return dk * scale, dv
 
 
-def kernel(tok, heads, dim, q_ref, g_ref, kv_ref, ends_ref, dq_out, term_ref, e_ref, dp_ref, m_ref, l_ref, t_ref, mc_ref, dq_ref):
+def kernel(tok, heads, dim, q_in, g_in, k_in, v_in, ends_in, dq_out, dk_out, dv_out, q_ref, g_ref, kv_ref, ends_ref, term_ref, sib_ref, yin_ref, home_ref, e_ref, dp_ref, m_ref, l_ref, t_ref, mc_ref, dq_ref, load_sem, ends_sem, direct_sem, relay_sem, core_sem, sib_sem, swap_sem, home_sem):
     scale = 1.0 / math.sqrt(dim)
     slope = scale * math.log2(math.e)
-    chunks = tok // CHUNK
     sizes = (tok, heads, dim, slope)
+    b = lax.axis_index("blk")
+    y = lax.axis_index("head")
+    count = lax.axis_size("blk")
+    core = lax.rem(b, 2)
+    sibling = b + 1 - 2 * core
+    mine = pl.ds(pl.multiple_of(y * CHUNK, CHUNK), CHUNK)
+    other = pl.ds(pl.multiple_of((1 - y) * CHUNK, CHUNK), CHUNK)
+    halves = (mine, other)
+    numbers = (y, 1 - y)
+
+    def at(shift):
+        return lax.rem(b + shift + count, count)
+
+    def remote(src, dst, send, recv, to_b, to_y):
+        return pltpu.make_async_remote_copy(
+            src_ref=src, dst_ref=dst, send_sem=send, recv_sem=recv,
+            device_id=(to_b, to_y), device_id_type=pl.DeviceIdType.MESH,
+        )
+
+    def ends_copy(d):
+        return remote(ends_ref.at[0], ends_ref.at[d], ends_sem.at[0, d], ends_sem.at[1, d], at(d), y)
+
+    def direct_copy(d):
+        i = d // 2
+        return remote(kv_ref.at[0, mine], kv_ref.at[d, mine], direct_sem.at[0, i], direct_sem.at[1, i], at(d), y)
+
+    def relay_copy(d, rows=mine):
+        i = d // 2
+        return remote(kv_ref.at[d, rows], kv_ref.at[d, rows], relay_sem.at[0, i], relay_sem.at[1, i], b, 1 - y)
+
+    def core_copy(slot, half):
+        rows = halves[half]
+        return remote(
+            kv_ref.at[slot - 1 + 2 * core, rows], kv_ref.at[slot, rows],
+            core_sem.at[0, slot, half], core_sem.at[1, slot, half], sibling, y,
+        )
+
+    def sib_copy(d, half):
+        rows = halves[half]
+        i = d // 2
+        return remote(term_ref.at[d, rows], sib_ref.at[i, rows], sib_sem.at[0, i, half], sib_sem.at[1, i, half], sibling, y)
+
+    def swap_copy(d):
+        i = d // 2
+        return remote(term_ref.at[d, other], yin_ref.at[i], swap_sem.at[0, i], swap_sem.at[1, i], b, 1 - y)
+
+    def home_copy(d):
+        i = d // 2 - 1
+        return remote(term_ref.at[d, mine], home_ref.at[i], home_sem.at[0, i], home_sem.at[1, i], at(-d), y)
+
+    loads = [
+        pltpu.make_async_copy(src, dst, load_sem.at[i])
+        for i, (src, dst) in enumerate(
+            [
+                (k_in, kv_ref.at[0, :, pl.ds(0, dim)]),
+                (v_in, kv_ref.at[0, :, pl.ds(dim, dim)]),
+                (ends_in, ends_ref.at[0]),
+                (q_in, q_ref),
+                (g_in, g_ref),
+            ]
+        )
+    ]
+    barrier = pltpu.get_barrier_semaphore()
+    for d in range(1, WINDOW + 1):
+        for shift in (d, -d):
+            pl.semaphore_signal(barrier, inc=1, device_id=(at(shift), y), device_id_type=pl.DeviceIdType.MESH)
+    pl.semaphore_signal(barrier, inc=1, device_id=(b, 1 - y), device_id_type=pl.DeviceIdType.MESH)
+    for load in loads:
+        load.start()
+    for load in loads[:3]:
+        load.wait()
+    pl.semaphore_wait(barrier, 2 * WINDOW + 1)
 
     def stats(d, r, q0=0, first=False):
         stats_step(d, r, q0, first, *sizes, q_ref, g_ref, kv_ref, ends_ref, e_ref, dp_ref, m_ref, l_ref, t_ref, mc_ref)
@@ -108,55 +179,174 @@
         term_ref[d, rows, 0:dim] = dk.astype(jnp.bfloat16)
         term_ref[d, rows, dim : 2 * dim] = dv.astype(jnp.bfloat16)
 
-    for r in range(chunks):
-        stats(0, r, r * CHUNK, r == 0)
-
+    def when(condition, run):
+        pl.when(condition)(run)
+
+    for d in (2, 4):
+        when(b + d < count, lambda d=d: direct_copy(d).start())
     for d in range(1, WINDOW + 1):
-
-        @pl.loop(0, chunks)
-        def _(r, d=d):
-            stats(d, r)
+        when(b + d < count, lambda d=d: ends_copy(d).start())
+
+    @pl.when(core == 0)
+    def _():
+        core_copy(1, 0).start()
+        core_copy(1, 1).start()
+
+    def pass_on(d, half):
+        if d == 2:
+            when((core == 0) & (sibling >= 3), lambda: core_copy(3, half).start())
+            when((core == 1) & (sibling >= 1), lambda: core_copy(1, half).start())
+        else:
+            when((core == 1) & (sibling >= 3), lambda: core_copy(3, half).start())
+
+    def direct_in(d):
+        @pl.when(b >= d)
+        def _():
+            direct_copy(d).wait_recv()
+            relay_copy(d).start()
+            pass_on(d, 0)
+
+    def relay_in(d):
+        @pl.when(b >= d)
+        def _():
+            relay_copy(d, other).wait_recv()
+            pass_on(d, 1)
+
+    def remote_stats(d, half):
+        @pl.when(b >= d)
+        def _():
+            if half == 0:
+                ends_copy(d).wait_recv()
+            if d % 2:
+                core_copy(d, half).wait_recv()
+            stats(d, numbers[half])
+
+    for d in (2, 4):
+
+        @pl.when(b + d >= count)
+        def _(d=d):
+            home_ref[d // 2 - 1] = jnp.zeros(home_ref.shape[1:], home_ref.dtype)
+
+    for load in loads[3:]:
+        load.wait()
+    stats(0, 0, 0, True)
+    direct_in(2)
+    stats(0, 1, CHUNK)
+    direct_in(4)
+    remote_stats(2, 0)
+    remote_stats(4, 0)
+    relay_in(2)
+    remote_stats(1, 0)
+    relay_in(4)
+    remote_stats(3, 0)
+    remote_stats(2, 1)
+    remote_stats(4, 1)
+    remote_stats(1, 1)
+    remote_stats(3, 1)
 
     inv = 1.0 / l_ref[...]
     l_ref[...] = inv
     t_ref[...] = t_ref[...] * inv
     dq_ref[...] = jnp.zeros_like(dq_ref)
-    for d in (4, 3, 2, 1):
-
-        @pl.loop(0, chunks)
-        def _(r, d=d):
-            grads(d, r)
-
-    for r in range(chunks):
-        grads(0, r, r * CHUNK)
+
+    def add(d, rows, part):
+        total = term_ref[d, rows, :].astype(jnp.float32) + part.astype(jnp.float32)
+        term_ref[d, rows, :] = total.astype(jnp.bfloat16)
+
+    def add_sibling(d, half):
+        rows = halves[half]
+
+        def take(source):
+            sib_copy(source, half).wait_recv()
+            add(d, rows, sib_ref[source // 2, rows, :])
+
+        if d == 4:
+            when(core == 1, lambda: take(3))
+        elif d == 2:
+            when(core == 0, lambda: take(3))
+            when(core == 1, lambda: take(1))
+        else:
+            when(core == 0, lambda: take(1))
+
+    def own_grads(half):
+        when(numbers[half] == 0, lambda: grads(0, 0))
+        when(numbers[half] == 1, lambda: grads(0, 1, CHUNK))
+        add_sibling(0, half)
+
+    for half in (1, 0):
+        for d in (3, 4, 1, 2):
+
+            @pl.when(b >= d)
+            def _(d=d, half=half):
+                grads(d, numbers[half])
+                if d % 2:
+                    sib_copy(d, half).start()
+                else:
+                    add_sibling(d, half)
+                    if half == 1:
+                        swap_copy(d).start()
+                    else:
+                        swap_copy(d).wait_recv()
+                        add(d, mine, yin_ref[d // 2])
+                        home_copy(d).start()
+
+        own_grads(half)
+        if half == 1:
+            swap_copy(0).start()
+
     for h in range(heads):
         dq_out[:, h * dim : (h + 1) * dim] = (dq_ref[h] * scale).T.astype(jnp.bfloat16)
-
-
-def passed_along(shard, axis, by):
-    count = lax.axis_size(axis)
-    pairs = [(i, i + by) for i in range(count) if 0 <= i + by < count]
-    return lax.ppermute(shard, axis, pairs)
+    total = term_ref[0, mine, :].astype(jnp.float32)
+    swap_copy(0).wait_recv()
+    total = total + yin_ref[0].astype(jnp.float32)
+    for d in (4, 2):
+        when(b + d < count, lambda d=d: home_copy(d).wait_recv())
+        total = total + home_ref[d // 2 - 1].astype(jnp.float32)
+    total = total.astype(jnp.bfloat16)
+    dk_out[...] = total[:, 0:dim]
+    dv_out[...] = total[:, dim : 2 * dim]
+    for d in range(1, WINDOW + 1):
+        when(b + d < count, lambda d=d: ends_copy(d).wait_send())
+    for d in (2, 4):
+        when(b + d < count, lambda d=d: direct_copy(d).wait_send())
+
+        @pl.when(b >= d)
+        def _(d=d):
+            relay_copy(d).wait_send()
+            swap_copy(d).wait_send()
+            home_copy(d).wait_send()
+
+    swap_copy(0).wait_send()
+    for d in (1, 3):
+        for half in (0, 1):
+            when(sibling >= d, lambda d=d, half=half: core_copy(d, half).wait_send())
+            when(b >= d, lambda d=d, half=half: sib_copy(d, half).wait_send())
 
 
 def body(query_rows, key_rows, value_rows, grad_out, subtree_end):
     tok, dim = key_rows.shape
     heads = query_rows.shape[1] // dim
-    kv = jnp.concatenate([key_rows, value_rows], axis=1)
     ends = subtree_end.reshape(tok // 128, 128)
-    kvs = [kv] + [passed_along(kv, "blk", d) for d in range(1, WINDOW + 1)]
-    end_list = [ends] + [passed_along(ends, "blk", d) for d in range(1, WINDOW + 1)]
     window = WINDOW + 1
     chunks = tok // CHUNK
-    dq, terms = pl.pallas_call(
+    return pl.pallas_call(
         functools.partial(kernel, tok, heads, dim),
         out_shape=(
             jax.ShapeDtypeStruct((tok, heads * dim), jnp.bfloat16),
-            jax.ShapeDtypeStruct((window, tok, 2 * dim), jnp.bfloat16),
+            jax.ShapeDtypeStruct((CHUNK, dim), jnp.bfloat16),
+            jax.ShapeDtypeStruct((CHUNK, dim), jnp.bfloat16),
         ),
-        in_specs=[pl.BlockSpec(memory_space=pltpu.VMEM)] * 4,
-        out_specs=[pl.BlockSpec(memory_space=pltpu.VMEM)] * 2,
+        in_specs=[pl.BlockSpec(memory_space=pl.ANY)] * 5,
+        out_specs=[pl.BlockSpec(memory_space=pltpu.VMEM)] * 3,
         scratch_shapes=[
+            pltpu.VMEM((tok, heads * dim), jnp.bfloat16),
+            pltpu.VMEM((tok, heads * dim), jnp.bfloat16),
+            pltpu.VMEM((window, tok, 2 * dim), jnp.bfloat16),
+            pltpu.VMEM((window, tok // 128, 128), jnp.int32),
+            pltpu.VMEM((window, tok, 2 * dim), jnp.bfloat16),
+            pltpu.VMEM((2, tok, 2 * dim), jnp.bfloat16),
+            pltpu.VMEM((3, CHUNK, 2 * dim), jnp.bfloat16),
+            pltpu.VMEM((2, CHUNK, 2 * dim), jnp.bfloat16),
             pltpu.VMEM((window * tok, heads * tok), jnp.bfloat16),
             pltpu.VMEM((window * tok, heads * tok), jnp.bfloat16),
             pltpu.VMEM((heads, tok), jnp.float32),
@@ -164,14 +354,19 @@
             pltpu.VMEM((heads, tok), jnp.float32),
             pltpu.VMEM((window * chunks, heads, tok), jnp.float32),
             pltpu.VMEM((heads, dim, tok), jnp.float32),
+            pltpu.SemaphoreType.DMA((5,)),
+            pltpu.SemaphoreType.DMA((2, window)),
+            pltpu.SemaphoreType.DMA((2, 3)),
+            pltpu.SemaphoreType.DMA((2, 3)),
+            pltpu.SemaphoreType.DMA((2, 4, 2)),
+            pltpu.SemaphoreType.DMA((2, 2, 2)),
+            pltpu.SemaphoreType.DMA((2, 3)),
+            pltpu.SemaphoreType.DMA((2, 2)),
         ],
-        compiler_params=pltpu.CompilerParams(vmem_limit_bytes=48 * 2**20),
-    )(query_rows, grad_out, jnp.stack(kvs), jnp.stack(end_list))
-    total = terms[0].astype(jnp.float32)
-    for d in range(1, window):
-        total = total + passed_along(terms[d], "blk", -d).astype(jnp.float32)
-    half = lax.psum_scatter(total.astype(jnp.bfloat16), "head", scatter_dimension=0, tiled=True)
-    return dq, half[:, :dim], half[:, dim:]
+        compiler_params=pltpu.CompilerParams(
+            vmem_limit_bytes=48 * 2**20, collective_id=0, has_side_effects=True
+        ),
+    )(query_rows, grad_out, key_rows, value_rows, ends)
 
 
 def solution(mesh):

time: 119 us -> 44 us (0.37)
  the two profiles are of different devices: /device:TPU:0 before, /device:TPU:2 now
where the time goes in v2:
time: 44 us; the launch traced here: 43.8 us
  Pallas kernels  36.5 us (83%)
  local copies, waits for them, and re-layouts  6.62 us (15%)
  between operations  0.65 us (1%)
    pallas_call x1, Pallas kernels, body(): pl.pallas_call(functools.partial(kernel, tok, heads, dim), out_shape=(jax...  36.5 us
    unnamed x13, local copies, waits for them, and re-layouts  6.62 us

profile of v2, /device:TPU:2, one launch (start us, length us, event | category | flops | bytes accessed | tf_op | source)
XLA Modules:
  0.0 43.8 jit_solution(17986587703134671375)
XLA Ops:
  0.6 0.0 copy-start
  0.6 1.0 %copy-done = bf16[512,512]{1,0:T(8,128)(2,1)S(1)} copy-done((bf16[512,512]{1,0:T(8,128)(2,1)S(1)}, bf16[512,512]{1,0:T(8,128)(2,1)}, u32[]{:S(2)}) %copy-start) | copy-done | bytes 524312
  1.7 0.0 copy-start.1
  1.7 1.0 %copy-done.1 = bf16[512,512]{1,0:T(8,128)(2,1)S(1)} copy-done((bf16[512,512]{1,0:T(8,128)(2,1)S(1)}, bf16[512,512]{1,0:T(8,128)(2,1)}, u32[]{:S(2)}) %copy-start.1) | copy-done | bytes 524312
  2.7 0.0 copy-start.2
  2.7 0.9 %copy-done.2 = bf16[512,128]{1,0:T(8,128)(2,1)S(1)} copy-done((bf16[512,128]{1,0:T(8,128)(2,1)S(1)}, bf16[512,128]{1,0:T(8,128)(2,1)}, u32[]{:S(2)}) %copy-start.2) | copy-done | bytes 131096
  3.6 0.0 copy-start.3
  3.6 0.9 %copy-done.3 = bf16[512,128]{1,0:T(8,128)(2,1)S(1)} copy-done((bf16[512,128]{1,0:T(8,128)(2,1)S(1)}, bf16[512,128]{1,0:T(8,128)(2,1)}, u32[]{:S(2)}) %copy-start.3) | copy-done | bytes 131096
  4.5 0.0 copy-start.4
  4.5 0.7 %copy-done.4 = s32[512]{0:T(512)S(1)} copy-done((s32[512]{0:T(512)S(1)}, s32[512]{0:T(512)}, u32[]{:S(2)}) %copy-start.4) | copy-done | bytes 2072
  5.2 36.5 %shard_map.76 = (bf16[512,512]{1,0:T(8,128)(2,1)S(1)}, bf16[256,128]{1,0:T(8,128)(2,1)S(1)}, bf16[256,128]{1,0:T(8,128)(2,1)S(1)}) custom-call(bf16[512,512]{1,0:T(8,128)(2,1)S(1)} %copy-done, bf16[512,512]{1,0:T(8,128)(2,1)S(1)} %copy-done.1, bf16[512,128]{1,0:T(8,128)(2,1)S(1)} %copy-done.2, bf16[512,128]{1,0:T(8,128)(2,1)S(1)} %copy-done.3, ...), custom_call_target="tpu_custom_call" | custom-call | tf_op jit(solution)/shard_map/pallas_call | solution.py:332
  41.7 0.8 %copy.11 = bf16[512,512]{1,0:T(8,128)(2,1)} copy(bf16[512,512]{1,0:T(8,128)(2,1)S(1)} %get-tuple-element.6) | data formatting | bytes 1048576
  42.5 0.6 %copy.12 = bf16[256,128]{1,0:T(8,128)(2,1)} copy(bf16[256,128]{1,0:T(8,128)(2,1)S(1)} %get-tuple-element.7) | data formatting | bytes 131072
  43.1 0.6 %copy.13 = bf16[256,128]{1,0:T(8,128)(2,1)} copy(bf16[256,128]{1,0:T(8,128)(2,1)S(1)} %get-tuple-element.8) | data formatting | bytes 131072
Async XLA Ops:
  0.6 1.0 %copy-start = (bf16[512,512]{1,0:T(8,128)(2,1)S(1)}, bf16[512,512]{1,0:T(8,128)(2,1)}, u32[]{:S(2)}) copy-start(bf16[512,512]{1,0:T(8,128)(2,1)} %q_in.1) | copy-start | bytes 1572868
  1.7 1.0 %copy-start.1 = (bf16[512,512]{1,0:T(8,128)(2,1)S(1)}, bf16[512,512]{1,0:T(8,128)(2,1)}, u32[]{:S(2)}) copy-start(bf16[512,512]{1,0:T(8,128)(2,1)} %g_in.1) | copy-start | bytes 1572868
  2.7 0.9 %copy-start.2 = (bf16[512,128]{1,0:T(8,128)(2,1)S(1)}, bf16[512,128]{1,0:T(8,128)(2,1)}, u32[]{:S(2)}) copy-start(bf16[512,128]{1,0:T(8,128)(2,1)} %k_in.1) | copy-start | bytes 393220
  3.6 0.9 %copy-start.3 = (bf16[512,128]{1,0:T(8,128)(2,1)S(1)}, bf16[512,128]{1,0:T(8,128)(2,1)}, u32[]{:S(2)}) copy-start(bf16[512,128]{1,0:T(8,128)(2,1)} %v_in.1) | copy-start | bytes 393220
  4.5 0.7 %copy-start.4 = (s32[512]{0:T(512)S(1)}, s32[512]{0:T(512)}, u32[]{:S(2)}) copy-start(s32[512]{0:T(512)} %param.9) | copy-start | bytes 6148
